TPU v7x, 32 devices: a whole 2x2x4 slice. The times are simulated.
32 devices in a mesh: tm: 4 (over x, core), fsdp: 8 (over z, y).
Axes of the slice: x: 2, y: 2, z: 4, core: 2. Of those that a mesh axis runs over, the one named last changes fastest.
Arguments:
- frames: bfloat16 [8, 2048, 512], P('fsdp', 'tm'), may hold values from -12 to 12
- retention: float32 [8, 2048, 512], P('fsdp', 'tm'), may hold values from 0.4 to 1
- first_conv: bfloat16 [1024, 1024], P('fsdp'), may hold values from -0.1875 to 0.1875
- second_conv: bfloat16 [1024, 1024], P('fsdp'), may hold values from -0.1875 to 0.1875
- cotangent: bfloat16 [8, 2048, 512], P('fsdp', 'tm'), may hold values from -0.125 to 0.125
Outputs:
- top_hidden: bfloat16 [8, 2048, 512], P('fsdp', 'tm')
- grad_first: float32 [1024, 1024], P('fsdp')
- grad_second: float32 [1024, 1024], P('fsdp')
All inputs are finite; a program needn't handle non-finite values.
Results may differ from a plain program's by a relative error of at most 0.035.
Values may be sent and summed in bfloat16 or wider, within the bound.
A program may use at most 128 MiB of HBM per device.

v0:
```python
import jax
import jax.numpy as jnp
from jax import lax
from jax.sharding import PartitionSpec as P


def prefix(part, axis, combine, identity):
    place = lax.axis_index(axis)
    gathered = jax.tree.map(lambda a: lax.all_gather(a, axis), part)
    state = jax.tree.map(lambda a, e: jnp.zeros_like(a) + jnp.asarray(e, a.dtype), part, identity)

    def one(step, state):
        return combine(
            state, jax.tree.map(lambda a: lax.dynamic_index_in_dim(a, step, 0, False), gathered)
        )

    return lax.fori_loop(0, place, one, state)


def passed_along(value, axis, steps):
    count = lax.axis_size(axis)
    leading, last = (max(0, -steps), min(count, count - steps))
    return lax.ppermute(value, axis, [(source, source + steps) for source in range(leading, last)])


def combine_maps(earlier, later):
    return (earlier[0] * later[0], later[0] * earlier[1] + later[1])


def gated(pre_values):
    split_at = pre_values.shape[1] // 2
    return jnp.tanh(pre_values[:, :split_at]) * jax.nn.sigmoid(pre_values[:, split_at:])


def gate_grad(pre_values, incoming_gradient):
    split_at = pre_values.shape[1] // 2
    tanh_part = jnp.tanh(pre_values[:, :split_at])
    gate_part = jax.nn.sigmoid(pre_values[:, split_at:])
    return jnp.concatenate(
        [
            incoming_gradient * gate_part * (1.0 - tanh_part * tanh_part),
            incoming_gradient * tanh_part * gate_part * (1.0 - gate_part),
        ],
        axis=1,
    )


def accumulate_with(operand, weights_block):
    return jnp.dot(operand, weights_block, preferred_element_type=jnp.float32)


def back_with(gradients, weights_block):
    return lax.dot_general(
        gradients, weights_block, (((1,), (1,)), ((), ())), preferred_element_type=jnp.float32
    )


def weight_term(operand, gradients):
    return lax.dot_general(
        operand, gradients, (((0,), (0,)), ((), ())), preferred_element_type=jnp.float32
    )


def on_device(frames, retention, first_conv, second_conv, cotangent):
    payload_elements = frames[0].astype(jnp.float32)
    keep_rate = retention[0]
    length, channels = payload_elements.shape
    short_lag = length // 4
    factor, local_part = lax.associative_scan(
        combine_maps, (keep_rate, (1.0 - keep_rate) * payload_elements), axis=0
    )
    identity_map = (jnp.ones((channels,), jnp.float32), jnp.zeros((channels,), jnp.float32))
    carried_in = prefix((factor[-1], local_part[-1]), "tm", combine_maps, identity_map)
    trend_removed = (payload_elements - (local_part + factor * carried_in[1][None, :])).astype(
        jnp.bfloat16
    )
    tail_rows = trend_removed[length - short_lag :]
    near_tail = passed_along(tail_rows, "tm", 1)
    own_past = jnp.concatenate([near_tail, trend_removed[: length - short_lag]], axis=0)
    opening_layer_input = jnp.concatenate([own_past, trend_removed], axis=1)
    stacked_pre = accumulate_with(
        opening_layer_input, lax.all_gather(first_conv, "fsdp", axis=0, tiled=True)
    )
    stacked_out = (trend_removed.astype(jnp.float32) + gated(stacked_pre)).astype(jnp.bfloat16)
    earlier_out = passed_along(stacked_out, "tm", 1)
    closing_layer_input = jnp.concatenate([earlier_out, stacked_out], axis=1)
    second_pre = accumulate_with(
        closing_layer_input, lax.all_gather(second_conv, "fsdp", axis=0, tiled=True)
    )
    top_hidden = (stacked_out.astype(jnp.float32) + gated(second_pre)).astype(jnp.bfloat16)
    incoming_gradient = cotangent[0].astype(jnp.float32)
    second_grad = gate_grad(second_pre, incoming_gradient).astype(jnp.bfloat16)
    second_shard = lax.psum_scatter(
        weight_term(closing_layer_input, second_grad).astype(jnp.bfloat16),
        "fsdp",
        scatter_dimension=0,
        tiled=True,
    )
    grad_second = lax.psum(second_shard, "tm").astype(jnp.float32)
    closing_backward = back_with(
        second_grad, lax.all_gather(second_conv, "fsdp", axis=0, tiled=True)
    )
    carried_back = passed_along(
        closing_backward[:, :channels].astype(jnp.bfloat16), "tm", -1
    ).astype(jnp.float32)
    opening_upstream_gradient = incoming_gradient + closing_backward[:, channels:] + carried_back
    first_grad = gate_grad(stacked_pre, opening_upstream_gradient).astype(jnp.bfloat16)
    first_shard = lax.psum_scatter(
        weight_term(opening_layer_input, first_grad).astype(jnp.bfloat16),
        "fsdp",
        scatter_dimension=0,
        tiled=True,
    )
    grad_first = lax.psum(first_shard, "tm").astype(jnp.float32)
    return (top_hidden[None], grad_first, grad_second)


def solution(mesh):
    in_specs = (
        P("fsdp", "tm", None),
        P("fsdp", "tm", None),
        P("fsdp", None),
        P("fsdp", None),
        P("fsdp", "tm", None),
    )
    out_specs = (P("fsdp", "tm", None), P("fsdp", None), P("fsdp", None))
    return jax.shard_map(
        on_device, mesh=mesh, in_specs=in_specs, out_specs=out_specs, check_vma=False
    )
```

profile of v0, /device:TPU:27, one launch (start us, length us, event | category | flops | bytes accessed | tf_op | source)
XLA Modules:
  0.0 300.1 jit_solution(827001314553152340)
XLA Ops:
  7.2 0.7 all-gather.5.cloned.1.call-update
  8.0 0.7 all-gather.7.cloned.1.call-update
  8.7 0.7 slice_bitcast_fusion
  9.4 3.0 slice.300
  12.4 3.7 %slice.299 = f32[255,512]{1,0:T(8,128)} slice(f32[512,512]{1,0:T(8,128)} %bitcast.39), slice={[2:512:2], [0:512:1]} | slice | bytes 1044480 | tf_op jit(solution)/shard_map/slice | solution.py:69
  16.1 2.1 slice.304
  18.4 2.1 slice.364
  20.5 2.1 slice.302
  22.6 2.1 slice.301
  24.7 1.4 multiply_add_fusion.1
  26.1 0.3 slice.362
  26.4 0.3 slice.308
  26.8 0.3 slice.307
  27.1 0.3 slice.310
  27.5 0.3 slice.306
  27.8 0.3 slice.305
  31.8 0.9 add.255
  32.7 0.9 add.245
  33.6 1.1 fusion.19
  34.9 0.5 slice-done
  35.4 0.4 copy-done.9
  36.0 2.3 pad.127
  38.3 5.6 %all-gather.1 = f32[4,1,512]{2,1,0:T(1,128)S(1)} all-gather(f32[1,1,512]{2,1,0:T(1,128)S(1)} %add_bitcast_fusion), channel_id=1, replica_groups=mesh['tm'=4,'fsdp'=8] {'tm'}, dimensions={0}, use_global_device_ids=true | all-gather | bytes 10240 | tf_op jit(solution)/shard_map/all_gather | solution.py:9
  43.9 4.6 %pad.145 = f32[512,512]{1,0:T(8,128)} pad(f32[256,512]{1,0:T(8,128)} %add.255, f32[]{:T(128)} %constant.23.clone.1), padding=1_0_1x0_0_0 | pad | bytes 1572868 | tf_op jit(solution)/shard_map/pad | solution.py:69
  48.6 0.7 add_bitcast_fusion.1
  49.3 5.2 %all-gather = f32[4,1,512]{2,1,0:T(1,128)S(1)} all-gather(f32[1,1,512]{2,1,0:T(1,128)S(1)} %add_bitcast_fusion.1), channel_id=1, replica_groups=mesh['tm'=4,'fsdp'=8] {'tm'}, dimensions={0}, use_global_device_ids=true | all-gather | bytes 10240 | tf_op jit(solution)/shard_map/all_gather | solution.py:9
  54.6 2.6 fusion
  57.2 1.3 collective-permute-start
  58.6 1.9 collective-permute-done
  60.5 2.9 fusion.20
  63.4 1.2 add_convert_fusion.1
  64.6 1.4 collective-permute-start.1
  66.0 42.8 %all-gather.7.cloned.1.call-done = bf16[1024,1024]{1,0:T(8,128)(2,1)} async-done(((bf16[128,1024]{1,0:T(8,128)(2,1)}), bf16[1024,1024]{1,0:T(8,128)(2,1)}) %all-gather.7.cloned.1.call-update) | async-done | bytes 2097168 | tf_op jit(solution)/shard_map/all_gather | solution.py:88
  108.8 3.2 %fusion.17 = f32[512,1024]{1,0:T(8,128)S(1)} fusion(bf16[1024,1024]{1,0:T(8,128)(2,1)} %all-gather.7.cloned.1.call-done, bf16[512,512]{1,0:T(8,128)(2,1)} %add_convert_fusion.1, bf16[512,512]{1,0:T(8,128)(2,1)} %collective-permute-done.1), kind=kOutput, calls=%fused_computation.39 | convolution fusion | flops 1075838976 | bytes 5242880 | tf_op jit(solution)/shard_map/dot_general | solution.py:49
  112.0 2.5 fusion.2
  114.5 0.8 copy-done.10
  115.4 3.8 %convolution_convert_fusion = bf16[1024,1024]{1,0:T(8,128)(2,1)} fusion(bf16[512,512]{1,0:T(8,128)(2,1)S(1)} %get-tuple-element.65, bf16[512,512]{1,0:T(8,128)(2,1)S(1)} %get-tuple-element.64, bf16[512,512]{1,0:T(8,128)(2,1)} %add_convert_fusion.1, bf16[512,512]{1,0:T(8,128)(2,1)} %collective-permute-done.1), kind=kOutput, calls=%fused_computation.3 | convolution fusion | flops 1078984704 | bytes 4194304 | tf_op jit(solution)/shard_map/dot_general | solution.py:59
  119.3 0.2 reduce-scatter.3.cloned.1.call-start
  119.5 3.2 %fusion.16 = f32[512,1024]{1,0:T(8,128)S(1)} fusion(bf16[1024,1024]{1,0:T(8,128)(2,1)} %all-gather.7.cloned.1.call-done, bf16[512,512]{1,0:T(8,128)(2,1)} %copy-done.11, bf16[512,512]{1,0:T(8,128)(2,1)} %copy-done.10), kind=kOutput, calls=%fused_computation.38 | convolution fusion | flops 1075838976 | bytes 5242880 | tf_op jit(solution)/shard_map/dot_general | solution.py:53
  122.8 2.8 collective-permute-start.2
  125.6 1.5 collective-permute-done.2
  127.1 0.6 multiply_convert_fusion.1
  127.8 2.6 convolution_convert_fusion.1
  130.5 53.9 %reduce-scatter.5.cloned.1.call-done = bf16[128,1024]{1,0:T(8,128)(2,1)} async-done(((bf16[1024,1024]{1,0:T(8,128)(2,1)}), bf16[128,1024]{1,0:T(8,128)(2,1)}) %reduce-scatter.5.cloned.1.call-update) | async-done | bytes 262160 | tf_op jit(solution)/shard_map/reduce_scatter | solution.py:93
  184.3 70.2 %reduce-scatter.3.cloned.1.call-done = bf16[128,1024]{1,0:T(8,128)(2,1)} async-done(((bf16[1024,1024]{1,0:T(8,128)(2,1)}), bf16[128,1024]{1,0:T(8,128)(2,1)}) %reduce-scatter.3.cloned.1.call-update) | async-done | bytes 262160 | tf_op jit(solution)/shard_map/reduce_scatter | solution.py:108
  254.5 35.4 %all-reduce.39.cloned.1.call-done = (bf16[128,1024]{1,0:T(8,128)(2,1)}, bf16[128,1024]{1,0:T(8,128)(2,1)}) async-done(((bf16[128,1024]{1,0:T(8,128)(2,1)}, bf16[128,1024]{1,0:T(8,128)(2,1)}), (bf16[128,1024]{1,0:T(8,128)(2,1)}, bf16[128,1024]{1,0:T(8,128)(2,1)})) %all-reduce.39.cloned.1.call-update) | async-done | bytes 524304 | tf_op jit(solution)/shard_map/psum | solution.py:114
  290.0 1.8 convert_element_type.56
  291.8 1.8 convert_element_type.58
  (170 shorter events, 4.3 us)
Async XLA Ops:
  7.2 9.0 %copy-start = (f32[1,512,512]{2,1,0:T(8,128)S(1)}, f32[1,512,512]{2,1,0:T(8,128)}, u32[]{:S(2)}) copy-start(f32[1,512,512]{2,1,0:T(8,128)} %param.8) | copy-start | bytes 3145732
  7.2 11.1 %copy-start.4 = (bf16[1,512,512]{2,1,0:T(8,128)(2,1)S(1)}, bf16[1,512,512]{2,1,0:T(8,128)(2,1)}, u32[]{:S(2)}) copy-start(bf16[1,512,512]{2,1,0:T(8,128)(2,1)} %param.7) | copy-start | bytes 1572868
  7.2 53.3 %all-gather.5.cloned.1.call-start = ((), (), s32[]{:S(2)}) async-start(), calls=%async_computation.2 | async-start | bytes 2359296 | tf_op jit(solution)/shard_map/all_gather | solution.py:82
  7.9 100.9 %all-gather.7.cloned.1.call-start = ((), (), s32[]{:S(2)}) async-start(), calls=%async_computation.3 | async-start | bytes 2359296 | tf_op jit(solution)/shard_map/all_gather | solution.py:88
  8.7 175.7 %reduce-scatter.5.cloned.1.call-start = ((), (), s32[]{:S(2)}) async-start(), calls=%async_computation.5 | async-start | bytes 2359296 | tf_op jit(solution)/shard_map/reduce_scatter | solution.py:93
  18.4 7.7 %copy-start.1 = (f32[512,512]{1,0:T(8,128)}, f32[512,512]{1,0:T(8,128)S(1)}, u32[]{:S(2)}) copy-start(f32[512,512]{1,0:T(8,128)S(1)} %convert_multiply_fusion.2) | copy-start | bytes 3145732
  18.4 6.3 %copy-start.6 = (f32[256,512]{1,0:T(8,128)S(1)}, f32[256,512]{1,0:T(8,128)}, u32[]{:S(2)}) copy-start(f32[256,512]{1,0:T(8,128)} %slice.304) | copy-start | bytes 1572868
  31.7 1.9 copy-start.7
  31.7 1.9 copy-start.8
  34.7 0.7 slice-start
  34.7 1.0 copy-start.9
  36.0 18.7 %copy-start.2 = (f32[512,512]{1,0:T(8,128)}, f32[512,512]{1,0:T(8,128)S(1)}, u32[]{:S(2)}) copy-start(f32[512,512]{1,0:T(8,128)S(1)} %pad.126) | copy-start | bytes 3145732
  38.3 16.4 %copy-start.3 = (f32[512,512]{1,0:T(8,128)}, f32[512,512]{1,0:T(8,128)S(1)}, u32[]{:S(2)}) copy-start(f32[512,512]{1,0:T(8,128)S(1)} %pad.127) | copy-start | bytes 3145732
  57.2 3.2 %collective-permute-start = (bf16[128,512]{1,0:T(8,128)(2,1)S(1)}, bf16[128,512]{1,0:T(8,128)(2,1)S(1)}, u32[]{:S(2)}, u32[]{:S(2)}) collective-permute-start(bf16[128,512]{1,0:T(8,128)(2,1)S(1)} %slice.450), channel_id=1, source_target_pairs={{0,8},{8,16},{16,24},{1,9},{9,17},{17,25},{2,10},{10,18},{18,26},{... | collective-permute-start | bytes 393224 | tf_op jit(solution)/shard_map/ppermute | solution.py:23
  60.5 2.9 copy-start.12
  64.6 47.4 %copy-start.5 = (bf16[1,512,512]{2,1,0:T(8,128)(2,1)S(1)}, bf16[1,512,512]{2,1,0:T(8,128)(2,1)}, u32[]{:S(2)}) copy-start(bf16[1,512,512]{2,1,0:T(8,128)(2,1)} %param.11) | copy-start | bytes 1572868
  64.6 44.2 %collective-permute-start.1 = (bf16[512,512]{1,0:T(8,128)(2,1)}, bf16[512,512]{1,0:T(8,128)(2,1)}, u32[]{:S(2)}, u32[]{:S(2)}) collective-permute-start(bf16[512,512]{1,0:T(8,128)(2,1)} %add_convert_fusion.1), channel_id=1, source_target_pairs={{0,8},{8,16},{16,24},{1,9},{9,17},{17,25},{2,10},{10,18},{18,26},{... | collective-permute-start | bytes 1572872 | tf_op jit(solution)/shard_map/ppermute | solution.py:23
  114.5 0.8 copy-start.10
  114.5 1.0 copy-start.11
  119.3 135.2 %reduce-scatter.3.cloned.1.call-start = ((), (), s32[]{:S(2)}) async-start(), calls=%async_computation.4 | async-start | bytes 2359296 | tf_op jit(solution)/shard_map/reduce_scatter | solution.py:108
  122.8 4.9 %copy-start.13 = (bf16[128,512]{1,0:T(8,128)(2,1)S(1)}, bf16[128,512]{1,0:T(8,128)(2,1)}, u32[]{:S(2)}) copy-start(bf16[128,512]{1,0:T(8,128)(2,1)} %copy-done.12) | copy-start | bytes 393220
  122.8 4.3 %collective-permute-start.2 = (bf16[512,512]{1,0:T(8,128)(2,1)S(1)}, bf16[512,512]{1,0:T(8,128)(2,1)S(1)}, u32[]{:S(2)}, u32[]{:S(2)}) collective-permute-start(bf16[512,512]{1,0:T(8,128)(2,1)S(1)} %slice.567), channel_id=1, source_target_pairs={{8,0},{16,8},{24,16},{9,1},{17,9},{25,17},{10,2},{18,10},{26,18},{... | collective-permute-start | bytes 1572872 | tf_op jit(solution)/shard_map/ppermute | solution.py:23
  130.4 159.5 %all-reduce.39.cloned.1.call-start = ((), (), s32[]{:S(2)}) async-start(), calls=%async_computation.6 | async-start | bytes 1048576 | tf_op jit(solution)/shard_map/psum | solution.py:114
Sparse Core Ops, SparseCore 0:
  10.1 48.6 all-gather.4
  61.0 47.7 all-gather.6
  119.4 64.8 reduce-scatter.4
  187.7 66.7 reduce-scatter.2
  256.8 33.1 all-reduce.38
where the time goes:
time: 304 us; the launch traced here: 300 us
  waiting for transfers between devices  207 us (68%)
  local copies, waits for them, and re-layouts  29.1 us (10%)
  other arithmetic  16.7 us (5%)
  matrix products  15.7 us (5%)
  between operations  14.8 us (5%)
  blocking collectives  10.8 us (4%)
  starting transfers between devices  5.89 us (2%)
    reduce_scatter x1, waiting for transfers between devices, on_device(): lax.psum_scatter(weight_term(opening_layer_input, first_grad).astype(jnp....  70.2 us
    reduce_scatter x1, waiting for transfers between devices, on_device(): lax.psum_scatter(weight_term(closing_layer_input, second_grad).astype(jnp...  53.9 us
    all_gather x1, waiting for transfers between devices, on_device(): lax.all_gather(second_conv, 'fsdp', axis=0, tiled=True)  42.8 us
    psum x1, waiting for transfers between devices, on_device(): grad_first = lax.psum(first_shard, 'tm').astype(jnp.float32)  35.4 us
    slice x61, local copies, waits for them, and re-layouts, on_device(): lax.associative_scan(combine_maps, (keep_rate, (1.0 - keep_rate) * payloa...  19.6 us
    all_gather x2, blocking collectives, prefix(): gathered = jax.tree.map(lambda a: lax.all_gather(a, axis), part)  10.8 us
    pad x32, local copies, waits for them, and re-layouts, on_device(): lax.associative_scan(combine_maps, (keep_rate, (1.0 - keep_rate) * payloa...  7.92 us
    dot_general x2, matrix products, weight_term(): lax.dot_general(operand, gradients, (((0,), (0,)), ((), ())), preferred_e...  6.44 us
  transfers between devices with their start and end apart: 8, of which 6 were waited for; matrix products, arithmetic and copies ran while one was open for 16% of the time, Pallas kernels for 0%

commit v1 on v0

--- a/solution.py
+++ b/solution.py
@@ -1,7 +1,14 @@
 import jax
 import jax.numpy as jnp
 from jax import lax
+from jax.experimental import pallas as pl
+from jax.experimental.pallas import tpu as pltpu
 from jax.sharding import PartitionSpec as P
+
+MESH = pl.DeviceIdType.MESH
+F32 = jnp.float32
+BF16 = jnp.bfloat16
+SEGS = 8
 
 
 def prefix(part, axis, combine, identity):
@@ -115,7 +122,368 @@
     return (top_hidden[None], grad_first, grad_second)
 
 
+def sigmoid(value):
+    return 0.5 * jnp.tanh(0.5 * value) + 0.5
+
+
+def kernel(
+    frames, keep, w1_hbm, w2_hbm, cot,
+    top, grad1, grad2,
+    xs, ks, hs, x1, tail_in, out1, prev_out, w1, w2,
+    th1, sg1, pre2, g, cb, cb_in,
+    ends, part, core_in, core_sum, x_in, x_sum, f_in, quarter,
+    local_sem, gs, gr, es, er, ns, nr, ss, sr, fs_s, fs_r, qs, qr,
+):
+    T, F = 4, 8
+    t, f = lax.axis_index("tm"), lax.axis_index("fsdp")
+    x, c = t // 2, t % 2
+    across = (1 - x) * 2 + c
+    sibling = x * 2 + (1 - c)
+    frames_n, ch = frames.shape
+    seg = frames_n // SEGS
+    lag = frames_n // 4
+    shard = w1_hbm.shape[0]
+    q = shard // T
+    pending = []
+
+    def rows(start, size):
+        return pl.ds(pl.multiple_of(start, size), size)
+
+    def send(src, dst, ssem, rsem, tm, fsdp):
+        copy = pltpu.make_async_remote_copy(
+            src_ref=src, dst_ref=dst, send_sem=ssem, recv_sem=rsem,
+            device_id=(tm, fsdp), device_id_type=MESH,
+        )
+        copy.start()
+        pending.append(copy)
+        return copy
+
+    own = [
+        pltpu.make_async_copy(wh, w.at[rows(f * shard, shard), :], local_sem.at[m])
+        for m, (wh, w) in enumerate(((w1_hbm, w1), (w2_hbm, w2)))
+    ]
+    for copy in own:
+        copy.start()
+
+    barrier = pltpu.get_barrier_semaphore()
+    for k in range(1, F):
+        pl.semaphore_signal(
+            barrier, inc=1, device_id=(t, lax.rem(f + k, F)), device_id_type=MESH
+        )
+    for k in range(1, T):
+        pl.semaphore_signal(
+            barrier, inc=1, device_id=(lax.rem(t + k, T), f), device_id_type=MESH
+        )
+    pl.semaphore_wait(barrier, F + T - 2)
+
+    def piece(w, owner, place):
+        return w.at[rows(owner * shard + place * q, q), :]
+
+    spread = [[], []]
+    for m, (wh, w) in enumerate(((w1_hbm, w1), (w2_hbm, w2))):
+        for k in range(1, F):
+            spread[m].append(
+                send(wh.at[rows(t * q, q), :], piece(w, f, t),
+                     gs.at[m, 0, k], gr.at[m, 0, k], t, lax.rem(f + k, F))
+            )
+
+    def complete(m, w):
+        over_x, over_core = [], []
+        for k in range(1, F):
+            owner = lax.rem(f + F - k, F)
+            spread[m][k - 1].wait_recv()
+            mine = piece(w, owner, t)
+            over_x.append(send(mine, mine, gs.at[m, 1, k], gr.at[m, 1, k], across, f))
+            over_core.append(send(mine, mine, gs.at[m, 2, k], gr.at[m, 2, k], sibling, f))
+        for k in range(1, F):
+            owner = lax.rem(f + F - k, F)
+            over_x[k - 1].wait_recv()
+            mine = piece(w, owner, across)
+            over_core.append(send(mine, mine, gs.at[m, 3, k], gr.at[m, 3, k], sibling, f))
+        for copy in over_core:
+            copy.wait_recv()
+        own[m].wait()
+
+    lanes = xs.shape[2]
+    groups = ch // lanes
+
+    @pl.loop(0, frames_n, step=64)
+    def _(r):
+        at = rows(r, 64)
+        for j in range(groups):
+            cols = pl.ds(j * lanes, lanes)
+            xs[j, at, :] = frames[at, cols].astype(F32)
+            ks[j, at, :] = keep[at, cols]
+
+    def step(i, state):
+        at = pl.ds(i, SEGS, stride=seg)
+        new = []
+        for j, (h, p) in enumerate(state):
+            a = ks[j, at, :]
+            h = a * h + (1.0 - a) * xs[j, at, :]
+            p = p * a
+            hs[j, at, :] = h
+            ks[j, at, :] = p
+            new.append((h, p))
+        return tuple(new)
+
+    nought = (jnp.zeros((SEGS, lanes), F32), jnp.ones((SEGS, lanes), F32))
+    lax.fori_loop(0, seg, step, (nought,) * groups, unroll=4)
+    before = []
+    for j in range(groups):
+        p, h = jnp.ones((1, lanes), F32), jnp.zeros((1, lanes), F32)
+        before.append([])
+        for s in range(SEGS):
+            before[j].append((p, h))
+            last = pl.ds((s + 1) * seg - 1, 1)
+            p, h = ks[j, last, :] * p, ks[j, last, :] * h + hs[j, last, :]
+        cols = pl.ds(j * lanes, lanes)
+        ends[t, 0:8, cols] = jnp.broadcast_to(p, (8, lanes))
+        ends[t, 8:16, cols] = jnp.broadcast_to(h, (8, lanes))
+    states = [
+        send(ends.at[t], ends.at[t], es.at[k], er.at[k], lax.rem(t + k, T), f)
+        for k in range(1, T)
+    ]
+    for copy in states:
+        copy.wait_recv()
+    carried = jnp.zeros((1, ch), F32)
+    for j in range(T):
+        pj = ends[j, 0:1, :]
+        hj = ends[j, 8:9, :]
+        carried = jnp.where(j < t, pj * carried + hj, carried)
+    for j in range(groups):
+        cols = slice(j * lanes, (j + 1) * lanes)
+        for s in range(SEGS):
+            pb, hb = before[j][s]
+            start = hb + pb * carried[:, cols]
+            at = pl.ds(s * seg, seg)
+            x1[at, ch + j * lanes : ch + (j + 1) * lanes] = (
+                xs[j, at, :] - (hs[j, at, :] + ks[j, at, :] * start)
+            ).astype(BF16)
+
+    def neighbour(src, dst, n, tm):
+        return pltpu.make_async_remote_copy(
+            src_ref=src, dst_ref=dst, send_sem=ns.at[n], recv_sem=nr.at[n],
+            device_id=(tm, f), device_id_type=MESH,
+        )
+
+    nxt, prv = lax.rem(t + 1, T), lax.rem(t + T - 1, T)
+    has_next, has_prev = t < T - 1, t > 0
+
+    tail = neighbour(x1.at[pl.ds(frames_n - lag, lag), pl.ds(ch, ch)], tail_in, 0, nxt)
+    pl.when(has_next)(tail.start)
+    x1[lag:, :ch] = x1[: frames_n - lag, ch:]
+
+    complete(0, w1)
+
+    @pl.when(has_prev)
+    def _():
+        tail.wait_recv()
+        x1[:lag, :ch] = tail_in[...]
+
+    @pl.when(t == 0)
+    def _():
+        x1[:lag, :ch] = jnp.zeros((lag, ch), BF16)
+
+    block = 128
+
+    @pl.loop(0, frames_n, step=block)
+    def _(r):
+        at = rows(r, block)
+        pre = jnp.dot(x1[at, :], w1[...], preferred_element_type=F32)
+        th, sg = jnp.tanh(pre[:, :ch]), sigmoid(pre[:, ch:])
+        th1[at, :] = th
+        sg1[at, :] = sg
+        out1[at, :] = (x1[at, ch:].astype(F32) + th * sg).astype(BF16)
+
+    passed = neighbour(out1, prev_out, 1, nxt)
+    pl.when(has_next)(passed.start)
+
+    complete(1, w2)
+
+    @pl.loop(0, frames_n, step=block)
+    def _(r):
+        at = rows(r, block)
+        pre2[at, :] = jnp.dot(out1[at, :], w2[ch:, :], preferred_element_type=F32)
+
+    @pl.when(has_prev)
+    def _():
+        passed.wait_recv()
+
+    @pl.when(t == 0)
+    def _():
+        prev_out[...] = jnp.zeros((frames_n, ch), BF16)
+
+    @pl.loop(0, frames_n, step=block)
+    def _(r):
+        at = rows(r, block)
+        pre = pre2[at, :] + jnp.dot(prev_out[at, :], w2[:ch, :], preferred_element_type=F32)
+        th, sg = jnp.tanh(pre[:, :ch]), sigmoid(pre[:, ch:])
+        u = cot[at, :].astype(F32)
+        top[at, :] = (out1[at, :].astype(F32) + th * sg).astype(BF16)
+        g2 = jnp.concatenate(
+            [u * sg * (1.0 - th * th), u * th * sg * (1.0 - sg)], axis=1
+        ).astype(BF16)
+        g[0, at, :] = g2
+        cb[at, :] = lax.dot_general(
+            g2, w2[:ch, :], (((1,), (1,)), ((), ())), preferred_element_type=F32
+        ).astype(BF16)
+
+    back = neighbour(cb, cb_in, 2, prv)
+    pl.when(has_prev)(back.start)
+
+    def partial(m, left, first_owner):
+        @pl.loop(0, ch // shard)
+        def _(j):
+            cols = pl.ds(pl.multiple_of(j * shard, shard), shard)
+            product = lax.dot_general(
+                left[:, cols], g[m], (((0,), (0,)), ((), ())), preferred_element_type=F32
+            )
+            part[m, first_owner + j] = product.astype(BF16).reshape(2, 2, q, 2 * ch)
+
+    def core_phase(m):
+        return send(part.at[m, :, :, 1 - c], core_in.at[m], ss.at[m, 0], sr.at[m, 0], sibling, f)
+
+    def x_phase(m, copy):
+        copy.wait_recv()
+
+        @pl.loop(0, F)
+        def _(j):
+            core_sum[m, j] = (
+                part[m, j, :, c].astype(F32) + core_in[m, j].astype(F32)
+            ).astype(BF16)
+
+        return send(core_sum.at[m, :, 1 - x], x_in.at[m], ss.at[m, 1], sr.at[m, 1], across, f)
+
+    def f_phase(m, copy):
+        copy.wait_recv()
+
+        @pl.loop(0, F)
+        def _(j):
+            x_sum[m, j] = (
+                core_sum[m, j, x].astype(F32) + x_in[m, j].astype(F32)
+            ).astype(BF16)
+
+        sends = []
+        for k in range(1, F):
+            to = lax.rem(f + k, F)
+            sends.append(
+                send(x_sum.at[m, to], f_in.at[m, k], fs_s.at[m, k], fs_r.at[m, k], t, to)
+            )
+        return sends
+
+    def q_phase(m, sends):
+        total = x_sum[m, f].astype(F32)
+        for k in range(1, F):
+            sends[k - 1].wait_recv()
+            total += f_in[m, k].astype(F32)
+        quarter[m, t] = total.astype(BF16)
+        return [
+            send(quarter.at[m, t], quarter.at[m, t], qs.at[m, k], qr.at[m, k],
+                 lax.rem(t + k, T), f)
+            for k in range(1, T)
+        ]
+
+    def finish(m, sends, grad):
+        for copy in sends:
+            copy.wait_recv()
+        for j in range(T):
+            grad[pl.ds(j * q, q), :] = quarter[m, j].astype(F32)
+
+    half = ch // shard
+    partial(0, prev_out, 0)
+    partial(0, out1, half)
+    core2 = core_phase(0)
+
+    @pl.loop(0, frames_n, step=block)
+    def _(r):
+        at = rows(r, block)
+        pre2[at, :ch] = cot[at, :].astype(F32) + lax.dot_general(
+            g[0, at, :], w2[ch:, :], (((1,), (1,)), ((), ())), preferred_element_type=F32
+        )
+
+    over2 = x_phase(0, core2)
+
+    @pl.when(has_next)
+    def _():
+        back.wait_recv()
+
+    @pl.when(t == T - 1)
+    def _():
+        cb_in[...] = jnp.zeros((frames_n, ch), BF16)
+
+    @pl.loop(0, frames_n, step=block)
+    def _(r):
+        at = rows(r, block)
+        u = pre2[at, :ch] + cb_in[at, :].astype(F32)
+        th, sg = th1[at, :], sg1[at, :]
+        g[1, at, :] = jnp.concatenate(
+            [u * sg * (1.0 - th * th), u * th * sg * (1.0 - sg)], axis=1
+        ).astype(BF16)
+
+    partial(1, x1.at[:, pl.ds(0, ch)], 0)
+    partial(1, x1.at[:, pl.ds(ch, ch)], half)
+    core1 = core_phase(1)
+    over1 = x_phase(1, core1)
+    spread2 = f_phase(0, over2)
+    spread1 = f_phase(1, over1)
+    last2 = q_phase(0, spread2)
+    last1 = q_phase(1, spread1)
+    finish(0, last2, grad2)
+    finish(1, last1, grad1)
+
+    for copy in pending:
+        copy.wait_send()
+    pl.when(has_next)(tail.wait_send)
+    pl.when(has_next)(passed.wait_send)
+    pl.when(has_prev)(back.wait_send)
+
+
+def fused(frames, retention, first_conv, second_conv, cotangent):
+    _, n, ch = frames.shape
+    shard, wide = first_conv.shape
+    T, F = 4, 8
+    q = shard // T
+    vm = lambda shape, dtype: pltpu.VMEM(shape, dtype)
+    dma = pltpu.SemaphoreType.DMA
+    vspec = pl.BlockSpec(memory_space=pltpu.VMEM)
+    anyspec = pl.BlockSpec(memory_space=pl.ANY)
+    top, grad1, grad2 = pl.pallas_call(
+        kernel,
+        out_shape=(
+            jax.ShapeDtypeStruct((n, ch), BF16),
+            jax.ShapeDtypeStruct((shard, wide), F32),
+            jax.ShapeDtypeStruct((shard, wide), F32),
+        ),
+        in_specs=[vspec, vspec, anyspec, anyspec, vspec],
+        out_specs=(vspec, vspec, vspec),
+        scratch_shapes=[
+            vm((ch // 128, n, 128), F32), vm((ch // 128, n, 128), F32), vm((ch // 128, n, 128), F32),
+            vm((n, wide), BF16), vm((n // 4, ch), BF16), vm((n, ch), BF16), vm((n, ch), BF16),
+            vm((wide, wide), BF16), vm((wide, wide), BF16),
+            vm((n, ch), F32), vm((n, ch), F32), vm((n, wide), F32),
+            vm((2, n, wide), BF16), vm((n, ch), BF16), vm((n, ch), BF16),
+            vm((T, 16, ch), F32),
+            vm((2, F, 2, 2, q, wide), BF16), vm((2, F, 2, q, wide), BF16),
+            vm((2, F, 2, q, wide), BF16), vm((2, F, q, wide), BF16),
+            vm((2, F, q, wide), BF16), vm((2, F, q, wide), BF16),
+            vm((2, T, q, wide), BF16),
+            dma((2,)), dma((2, 4, F)), dma((2, 4, F)), dma((T,)), dma((T,)),
+            dma((3,)), dma((3,)), dma((2, 2)), dma((2, 2)),
+            dma((2, F)), dma((2, F)), dma((2, T)), dma((2, T)),
+        ],
+        compiler_params=pltpu.CompilerParams(
+            collective_id=0, has_side_effects=True, vmem_limit_bytes=56 * 2**20
+        ),
+        cost_estimate=pl.CostEstimate(
+            flops=10 * n * wide * wide, bytes_accessed=8 * n * wide, transcendentals=2 * n * wide
+        ),
+    )(frames[0], retention[0], first_conv, second_conv, cotangent[0])
+    return (top[None], grad1, grad2)
+
+
 def solution(mesh):
+    fits = mesh.shape["tm"] == 4 and mesh.shape["fsdp"] == 8
     in_specs = (
         P("fsdp", "tm", None),
         P("fsdp", "tm", None),
@@ -125,5 +493,9 @@
     )
     out_specs = (P("fsdp", "tm", None), P("fsdp", None), P("fsdp", None))
     return jax.shard_map(
-        on_device, mesh=mesh, in_specs=in_specs, out_specs=out_specs, check_vma=False
-    )
+        fused if fits else on_device,
+        mesh=mesh,
+        in_specs=in_specs,
+        out_specs=out_specs,
+        check_vma=False,
+    )

time: 304 us -> 107 us (0.35); the launches traced: 300 us -> 107 us
  waiting for transfers between devices: 207 us -> 0 us
  Pallas kernels: 0 us -> 102 us
  local copies, waits for them, and re-layouts: 29.1 us -> 3.95 us
  other arithmetic: 16.7 us -> 0 us
  matrix products: 15.7 us -> 0 us
  between operations: 14.8 us -> 0.65 us
  blocking collectives: 10.8 us -> 0 us
  starting transfers between devices: 5.89 us -> 0 us
    reduce_scatter x2 -> x0, waiting for transfers between devices: 124 us -> none  [the longest x1 70.2 us: on_device(): lax.psum_scatter(weight_term(opening_layer_input, first_grad).astype(jnp....]
    pallas_call x0 -> x1, Pallas kernels: none -> 102 us  [fused(): pl.pallas_call(kernel, out_shape=(jax.ShapeDtypeStruct((n, ch), BF16), ja...]
    all_gather x2 -> x0, waiting for transfers between devices: 42.8 us -> none  [the longest x1 42.8 us: on_device(): lax.all_gather(second_conv, 'fsdp', axis=0, tiled=True)]
    psum x1 -> x0, waiting for transfers between devices: 35.4 us -> none  [on_device(): grad_first = lax.psum(first_shard, 'tm').astype(jnp.float32)]
    slice x64 -> x0, local copies, waits for them, and re-layouts: 19.7 us -> none  [the longest x61 19.6 us: on_device(): lax.associative_scan(combine_maps, (keep_rate, (1.0 - keep_rate) * payloa...]
    dot_general x5 -> x0, matrix products: 15.7 us -> none  [the longest x2 6.44 us: weight_term(): lax.dot_general(operand, gradients, (((0,), (0,)), ((), ())), preferred_e...]
    all_gather x2 -> x0, blocking collectives: 10.8 us -> none  [prefix(): gathered = jax.tree.map(lambda a: lax.all_gather(a, axis), part)]
    pad x32 -> x0, local copies, waits for them, and re-layouts: 7.92 us -> none  [on_device(): lax.associative_scan(combine_maps, (keep_rate, (1.0 - keep_rate) * payloa...]
  transfers between devices with their start and end apart: 8 -> 0, of which waited for: 6 -> 0; matrix products, arithmetic and copies ran while one was open for 16% -> 0% of each run, Pallas kernels for 0% -> 0%
where the time goes in v1:
time: 107 us
  Pallas kernels  102 us (95%)
  local copies, waits for them, and re-layouts  3.95 us (4%)
    pallas_call x1, Pallas kernels, fused(): pl.pallas_call(kernel, out_shape=(jax.ShapeDtypeStruct((n, ch), BF16), ja...  102 us
    unnamed x7, local copies, waits for them, and re-layouts  3.95 us

profile of v1, /device:TPU:27, one launch (start us, length us, event | category | flops | bytes accessed | tf_op | source)
XLA Modules:
  0.0 106.9 jit_solution(13087282436823636847)
XLA Ops:
  0.6 102.3 %shard_map.76 = (bf16[512,512]{1,0:T(8,128)(2,1)}, f32[128,1024]{1,0:T(8,128)}, f32[128,1024]{1,0:T(8,128)}) custom-call(bf16[512,512]{1,0:T(8,128)(2,1)} %bitcast.6, f32[512,512]{1,0:T(8,128)} %bitcast.5, bf16[128,1024]{1,0:T(8,128)(2,1)} %w1_hbm.1, bf16[128,1024]{1,0:T(8,128)(2,1)} %w2_hbm.1, bf16[512,512]{1,0:T(8,128)(2,1)} %bitcast.7), custom_call_target="tpu_custom_call" | custom-call | flops 5368709120 | bytes 4194304 | tf_op jit(solution)/shard_map/pallas_call | solution.py:451
  102.9 0.0 copy-start.1
  102.9 1.9 %copy.11 = bf16[1,512,512]{2,1,0:T(8,128)(2,1)} copy(bf16[1,512,512]{2,1,0:T(8,128)(2,1)} %bitcast.4) | data formatting | bytes 1048576
  104.8 0.0 copy-done.1
  104.8 0.0 copy-start
  104.8 0.8 copy.12
  105.6 0.4 copy-done
  106.1 0.8 copy.13
Async XLA Ops:
  102.9 1.9 %copy-start.1 = (f32[128,1024]{1,0:T(8,128)S(1)}, f32[128,1024]{1,0:T(8,128)}, u32[]{:S(2)}) copy-start(f32[128,1024]{1,0:T(8,128)} %get-tuple-element.13) | copy-start | bytes 1572868
  104.8 1.2 %copy-start = (f32[128,1024]{1,0:T(8,128)S(1)}, f32[128,1024]{1,0:T(8,128)}, u32[]{:S(2)}) copy-start(f32[128,1024]{1,0:T(8,128)} %get-tuple-element.14) | copy-start | bytes 1572868

commit v2 on v1

--- a/solution.py
+++ b/solution.py
@@ -131,14 +131,17 @@
     top, grad1, grad2,
     xs, ks, hs, x1, tail_in, out1, prev_out, w1, w2,
     th1, sg1, pre2, g, cb, cb_in,
-    ends, part, core_in, core_sum, x_in, x_sum, f_in, quarter,
-    local_sem, gs, gr, es, er, ns, nr, ss, sr, fs_s, fs_r, qs, qr,
+    ends, part, core_in, core_sum, a_in, a_sum, b_in, b_sum, z_in, quarter,
+    local_sem, gs, gr, es, er, ns, nr, os, orr, bs, br, ss, sr, zs, zr, qs, qr,
 ):
     T, F = 4, 8
     t, f = lax.axis_index("tm"), lax.axis_index("fsdp")
     x, c = t // 2, t % 2
+    z, y = f // 2, f % 2
+    place = c * 2 + x
     across = (1 - x) * 2 + c
     sibling = x * 2 + (1 - c)
+    over_y = z * 2 + (1 - y)
     frames_n, ch = frames.shape
     seg = frames_n // SEGS
     lag = frames_n // 4
@@ -176,33 +179,38 @@
         )
     pl.semaphore_wait(barrier, F + T - 2)
 
-    def piece(w, owner, place):
-        return w.at[rows(owner * shard + place * q, q), :]
-
-    spread = [[], []]
-    for m, (wh, w) in enumerate(((w1_hbm, w1), (w2_hbm, w2))):
-        for k in range(1, F):
-            spread[m].append(
-                send(wh.at[rows(t * q, q), :], piece(w, f, t),
-                     gs.at[m, 0, k], gr.at[m, 0, k], t, lax.rem(f + k, F))
-            )
-
-    def complete(m, w):
-        over_x, over_core = [], []
-        for k in range(1, F):
-            owner = lax.rem(f + F - k, F)
-            spread[m][k - 1].wait_recv()
-            mine = piece(w, owner, t)
-            over_x.append(send(mine, mine, gs.at[m, 1, k], gr.at[m, 1, k], across, f))
-            over_core.append(send(mine, mine, gs.at[m, 2, k], gr.at[m, 2, k], sibling, f))
-        for k in range(1, F):
-            owner = lax.rem(f + F - k, F)
-            over_x[k - 1].wait_recv()
-            mine = piece(w, owner, across)
-            over_core.append(send(mine, mine, gs.at[m, 3, k], gr.at[m, 3, k], sibling, f))
-        for copy in over_core:
-            copy.wait_recv()
-        own[m].wait()
+    half_rows = 2 * q
+    Z = F // 2
+    weights = (w1, w2)
+
+    def quarter_of(w, owner, at):
+        return w.at[rows(owner * shard + at * q, q), :]
+
+    def half_of(w, owner):
+        return w.at[rows(owner * shard + c * half_rows, half_rows), :]
+
+    def hop(m, stage, k, src, dst, tm, fsdp):
+        return send(src, dst, gs.at[m, stage, k], gr.at[m, stage, k], tm, fsdp)
+
+    def zone(k):
+        return lax.rem(z + Z - k, Z)
+
+    def at_z(k):
+        return lax.rem(z + k, Z) * 2 + y
+
+    along = [
+        [
+            hop(m, 0, k, wh.at[rows(place * q, q), :], quarter_of(w, f, place), t, at_z(k))
+            for k in range(1, Z)
+        ]
+        for m, (wh, w) in enumerate(((w1_hbm, w1), (w2_hbm, w2)))
+    ]
+    first_y = [
+        hop(0, 2, 0, w1_hbm.at[rows(c * half_rows, half_rows), :], half_of(w1, f), t, over_y)
+    ]
+    second_y = [
+        hop(1, 1, 0, w2_hbm.at[rows(place * q, q), :], quarter_of(w2, f, place), t, over_y)
+    ]
 
     lanes = xs.shape[2]
     groups = ch // lanes
@@ -244,6 +252,15 @@
         send(ends.at[t], ends.at[t], es.at[k], er.at[k], lax.rem(t + k, T), f)
         for k in range(1, T)
     ]
+    first_x = []
+    for k in range(1, Z):
+        along[0][k - 1].wait_recv()
+        mine = quarter_of(w1, zone(k) * 2 + y, place)
+        first_x.append(hop(0, 1, k, mine, mine, across, f))
+    for k in range(1, Z):
+        along[1][k - 1].wait_recv()
+        mine = quarter_of(w2, zone(k) * 2 + y, place)
+        second_y.append(hop(1, 1, k, mine, mine, t, over_y))
     for copy in states:
         copy.wait_recv()
     carried = jnp.zeros((1, ch), F32)
@@ -274,7 +291,26 @@
     pl.when(has_next)(tail.start)
     x1[lag:, :ch] = x1[: frames_n - lag, ch:]
 
-    complete(0, w1)
+    first_core, second_x, second_core = [], [], []
+    for k in range(1, Z):
+        first_x[k - 1].wait_recv()
+        mine = half_of(w1, zone(k) * 2 + y)
+        first_y.append(hop(0, 2, k, mine, mine, t, over_y))
+        first_core.append(hop(0, 3, k, mine, mine, sibling, f))
+    for k in range(1, Z):
+        mine = quarter_of(w2, zone(k) * 2 + y, place)
+        second_x.append(hop(1, 2, k, mine, mine, across, f))
+    for k in range(Z):
+        second_y[k].wait_recv()
+        mine = quarter_of(w2, zone(k) * 2 + 1 - y, place)
+        second_x.append(hop(1, 2, Z + k, mine, mine, across, f))
+    for k in range(Z):
+        first_y[k].wait_recv()
+        mine = half_of(w1, zone(k) * 2 + 1 - y)
+        first_core.append(hop(0, 3, Z + k, mine, mine, sibling, f))
+    for copy in first_core:
+        copy.wait_recv()
+    own[0].wait()
 
     @pl.when(has_prev)
     def _():
@@ -286,6 +322,20 @@
         x1[:lag, :ch] = jnp.zeros((lag, ch), BF16)
 
     block = 128
+
+    def blockwise(src, dst, ssems, rsems, tm):
+        def copy(r):
+            at = rows(r, block)
+            return pltpu.make_async_remote_copy(
+                src_ref=src.at[at, :], dst_ref=dst.at[at, :],
+                send_sem=ssems.at[r // block], recv_sem=rsems.at[r // block],
+                device_id=(tm, f), device_id_type=MESH,
+            )
+
+        return copy
+
+    passed = blockwise(out1, prev_out, os, orr, nxt)
+    back = blockwise(cb, cb_in, bs, br, prv)
 
     @pl.loop(0, frames_n, step=block)
     def _(r):
@@ -296,28 +346,35 @@
         sg1[at, :] = sg
         out1[at, :] = (x1[at, ch:].astype(F32) + th * sg).astype(BF16)
 
-    passed = neighbour(out1, prev_out, 1, nxt)
-    pl.when(has_next)(passed.start)
-
-    complete(1, w2)
+        @pl.when(has_next)
+        def _():
+            passed(r).start()
+
+    for k in range(2 * Z - 1):
+        second_x[k].wait_recv()
+        owner = zone(k + 1) * 2 + y if k < Z - 1 else zone(k - Z + 1) * 2 + 1 - y
+        mine = half_of(w2, owner)
+        second_core.append(hop(1, 3, k, mine, mine, sibling, f))
+
+    @pl.when(t == 0)
+    def _():
+        prev_out[...] = jnp.zeros((frames_n, ch), BF16)
+
+    for copy in second_core:
+        copy.wait_recv()
+    own[1].wait()
 
     @pl.loop(0, frames_n, step=block)
     def _(r):
         at = rows(r, block)
-        pre2[at, :] = jnp.dot(out1[at, :], w2[ch:, :], preferred_element_type=F32)
-
-    @pl.when(has_prev)
-    def _():
-        passed.wait_recv()
-
-    @pl.when(t == 0)
-    def _():
-        prev_out[...] = jnp.zeros((frames_n, ch), BF16)
-
-    @pl.loop(0, frames_n, step=block)
-    def _(r):
-        at = rows(r, block)
-        pre = pre2[at, :] + jnp.dot(prev_out[at, :], w2[:ch, :], preferred_element_type=F32)
+
+        @pl.when(has_prev)
+        def _():
+            passed(r).wait_recv()
+
+        pre = jnp.dot(out1[at, :], w2[ch:, :], preferred_element_type=F32) + jnp.dot(
+            prev_out[at, :], w2[:ch, :], preferred_element_type=F32
+        )
         th, sg = jnp.tanh(pre[:, :ch]), sigmoid(pre[:, ch:])
         u = cot[at, :].astype(F32)
         top[at, :] = (out1[at, :].astype(F32) + th * sg).astype(BF16)
@@ -329,8 +386,9 @@
             g2, w2[:ch, :], (((1,), (1,)), ((), ())), preferred_element_type=F32
         ).astype(BF16)
 
-    back = neighbour(cb, cb_in, 2, prv)
-    pl.when(has_prev)(back.start)
+        @pl.when(has_prev)
+        def _():
+            back(r).start()
 
     def partial(m, left, first_owner):
         @pl.loop(0, ch // shard)
@@ -339,47 +397,68 @@
             product = lax.dot_general(
                 left[:, cols], g[m], (((0,), (0,)), ((), ())), preferred_element_type=F32
             )
-            part[m, first_owner + j] = product.astype(BF16).reshape(2, 2, q, 2 * ch)
-
-    def core_phase(m):
-        return send(part.at[m, :, :, 1 - c], core_in.at[m], ss.at[m, 0], sr.at[m, 0], sibling, f)
-
-    def x_phase(m, copy):
+            owner = first_owner + j
+            part[m, owner // 2, owner % 2] = product.astype(BF16).reshape(2, 2, q, 2 * ch)
+
+    two = Z // 2
+
+    def span(h):
+        return pl.ds(h * two, two)
+
+    def core_phase(m, h):
+        return send(part.at[m, span(h), :, 1 - c], core_in.at[m, span(h)],
+                    ss.at[m, 0, h], sr.at[m, 0, h], sibling, f)
+
+    def a_phase(m, h, copy):
         copy.wait_recv()
-
-        @pl.loop(0, F)
-        def _(j):
-            core_sum[m, j] = (
-                part[m, j, :, c].astype(F32) + core_in[m, j].astype(F32)
+        for j in range(h * two, (h + 1) * two):
+            for d in range(2):
+                for e in range(2):
+                    yy, xx = (d, e) if m == 0 else (e, d)
+                    core_sum[m, d, j, e] = (
+                        part[m, j, yy, c, xx].astype(F32) + core_in[m, j, yy, xx].astype(F32)
+                    ).astype(BF16)
+        mine, tm, fsdp = (y, t, over_y) if m == 0 else (x, across, f)
+        return send(core_sum.at[m, 1 - mine, span(h)], a_in.at[m, span(h)],
+                    ss.at[m, 1, h], sr.at[m, 1, h], tm, fsdp)
+
+    def b_phase(m, h, copy):
+        copy.wait_recv()
+        mine = y if m == 0 else x
+        for j in range(h * two, (h + 1) * two):
+            for e in range(2):
+                a_sum[m, e, j] = (
+                    core_sum[m, mine, j, e].astype(F32) + a_in[m, j, e].astype(F32)
+                ).astype(BF16)
+        mine, tm, fsdp = (x, across, f) if m == 0 else (y, t, over_y)
+        return send(a_sum.at[m, 1 - mine, span(h)], b_in.at[m, span(h)],
+                    ss.at[m, 2, h], sr.at[m, 2, h], tm, fsdp)
+
+    def z_copy(m, j, source):
+        return pltpu.make_async_remote_copy(
+            src_ref=b_sum.at[m, j], dst_ref=z_in.at[m, source],
+            send_sem=zs.at[m, j], recv_sem=zr.at[m, source],
+            device_id=(t, j * 2 + y), device_id_type=MESH,
+        )
+
+    def z_phase(m, h, copy):
+        copy.wait_recv()
+        mine = x if m == 0 else y
+        for j in range(h * two, (h + 1) * two):
+            b_sum[m, j] = (
+                a_sum[m, mine, j].astype(F32) + b_in[m, j].astype(F32)
             ).astype(BF16)
-
-        return send(core_sum.at[m, :, 1 - x], x_in.at[m], ss.at[m, 1], sr.at[m, 1], across, f)
-
-    def f_phase(m, copy):
-        copy.wait_recv()
-
-        @pl.loop(0, F)
-        def _(j):
-            x_sum[m, j] = (
-                core_sum[m, j, x].astype(F32) + x_in[m, j].astype(F32)
-            ).astype(BF16)
-
-        sends = []
-        for k in range(1, F):
-            to = lax.rem(f + k, F)
-            sends.append(
-                send(x_sum.at[m, to], f_in.at[m, k], fs_s.at[m, k], fs_r.at[m, k], t, to)
-            )
-        return sends
-
-    def q_phase(m, sends):
-        total = x_sum[m, f].astype(F32)
-        for k in range(1, F):
-            sends[k - 1].wait_recv()
-            total += f_in[m, k].astype(F32)
-        quarter[m, t] = total.astype(BF16)
+            pl.when(z != j)(z_copy(m, j, z).start)
+
+    def q_phase(m):
+        total = b_sum[m, z].astype(F32)
+        for k in range(1, Z):
+            source = zone(k)
+            z_copy(m, k, source).wait_recv()
+            total += z_in[m, source].astype(F32)
+        quarter[m, place] = total.astype(BF16)
         return [
-            send(quarter.at[m, t], quarter.at[m, t], qs.at[m, k], qr.at[m, k],
+            send(quarter.at[m, place], quarter.at[m, place], qs.at[m, k], qr.at[m, k],
                  lax.rem(t + k, T), f)
             for k in range(1, T)
         ]
@@ -392,21 +471,19 @@
 
     half = ch // shard
     partial(0, prev_out, 0)
+    core20 = core_phase(0, 0)
     partial(0, out1, half)
-    core2 = core_phase(0)
+    core21 = core_phase(0, 1)
+    a20 = a_phase(0, 0, core20)
 
     @pl.loop(0, frames_n, step=block)
     def _(r):
         at = rows(r, block)
-        pre2[at, :ch] = cot[at, :].astype(F32) + lax.dot_general(
+        pre2[at, :] = cot[at, :].astype(F32) + lax.dot_general(
             g[0, at, :], w2[ch:, :], (((1,), (1,)), ((), ())), preferred_element_type=F32
         )
 
-    over2 = x_phase(0, core2)
-
-    @pl.when(has_next)
-    def _():
-        back.wait_recv()
+    a21 = a_phase(0, 1, core21)
 
     @pl.when(t == T - 1)
     def _():
@@ -415,34 +492,51 @@
     @pl.loop(0, frames_n, step=block)
     def _(r):
         at = rows(r, block)
-        u = pre2[at, :ch] + cb_in[at, :].astype(F32)
+
+        @pl.when(has_next)
+        def _():
+            back(r).wait_recv()
+
+        u = pre2[at, :] + cb_in[at, :].astype(F32)
         th, sg = th1[at, :], sg1[at, :]
         g[1, at, :] = jnp.concatenate(
             [u * sg * (1.0 - th * th), u * th * sg * (1.0 - sg)], axis=1
         ).astype(BF16)
 
     partial(1, x1.at[:, pl.ds(0, ch)], 0)
+    core10 = core_phase(1, 0)
     partial(1, x1.at[:, pl.ds(ch, ch)], half)
-    core1 = core_phase(1)
-    over1 = x_phase(1, core1)
-    spread2 = f_phase(0, over2)
-    spread1 = f_phase(1, over1)
-    last2 = q_phase(0, spread2)
-    last1 = q_phase(1, spread1)
+    core11 = core_phase(1, 1)
+    a10 = a_phase(1, 0, core10)
+    a11 = a_phase(1, 1, core11)
+    b20 = b_phase(0, 0, a20)
+    b21 = b_phase(0, 1, a21)
+    b10 = b_phase(1, 0, a10)
+    z_phase(0, 0, b20)
+    z_phase(0, 1, b21)
+    b11 = b_phase(1, 1, a11)
+    z_phase(1, 0, b10)
+    z_phase(1, 1, b11)
+    last2 = q_phase(0)
+    last1 = q_phase(1)
     finish(0, last2, grad2)
     finish(1, last1, grad1)
 
     for copy in pending:
         copy.wait_send()
+    for m in range(2):
+        for j in range(Z):
+            pl.when(z != j)(z_copy(m, j, z).wait_send)
     pl.when(has_next)(tail.wait_send)
-    pl.when(has_next)(passed.wait_send)
-    pl.when(has_prev)(back.wait_send)
+    for r in range(0, frames_n, block):
+        pl.when(has_next)(passed(r).wait_send)
+        pl.when(has_prev)(back(r).wait_send)
 
 
 def fused(frames, retention, first_conv, second_conv, cotangent):
     _, n, ch = frames.shape
     shard, wide = first_conv.shape
-    T, F = 4, 8
+    T, F, Z = 4, 8, 4
     q = shard // T
     vm = lambda shape, dtype: pltpu.VMEM(shape, dtype)
     dma = pltpu.SemaphoreType.DMA
@@ -461,16 +555,18 @@
             vm((ch // 128, n, 128), F32), vm((ch // 128, n, 128), F32), vm((ch // 128, n, 128), F32),
             vm((n, wide), BF16), vm((n // 4, ch), BF16), vm((n, ch), BF16), vm((n, ch), BF16),
             vm((wide, wide), BF16), vm((wide, wide), BF16),
-            vm((n, ch), F32), vm((n, ch), F32), vm((n, wide), F32),
+            vm((n, ch), F32), vm((n, ch), F32), vm((n, ch), F32),
             vm((2, n, wide), BF16), vm((n, ch), BF16), vm((n, ch), BF16),
             vm((T, 16, ch), F32),
-            vm((2, F, 2, 2, q, wide), BF16), vm((2, F, 2, q, wide), BF16),
-            vm((2, F, 2, q, wide), BF16), vm((2, F, q, wide), BF16),
-            vm((2, F, q, wide), BF16), vm((2, F, q, wide), BF16),
+            vm((2, Z, 2, 2, 2, q, wide), BF16), vm((2, Z, 2, 2, q, wide), BF16),
+            vm((2, 2, Z, 2, q, wide), BF16), vm((2, Z, 2, q, wide), BF16),
+            vm((2, 2, Z, q, wide), BF16), vm((2, Z, q, wide), BF16),
+            vm((2, Z, q, wide), BF16), vm((2, Z, q, wide), BF16),
             vm((2, T, q, wide), BF16),
             dma((2,)), dma((2, 4, F)), dma((2, 4, F)), dma((T,)), dma((T,)),
-            dma((3,)), dma((3,)), dma((2, 2)), dma((2, 2)),
-            dma((2, F)), dma((2, F)), dma((2, T)), dma((2, T)),
+            dma((1,)), dma((1,)), dma((4,)), dma((4,)), dma((4,)), dma((4,)),
+            dma((2, 3, 2)), dma((2, 3, 2)), dma((2, Z)), dma((2, Z)),
+            dma((2, T)), dma((2, T)),
         ],
         compiler_params=pltpu.CompilerParams(
             collective_id=0, has_side_effects=True, vmem_limit_bytes=56 * 2**20

time: 107 us -> 91 us (0.85)
  Pallas kernels: 102 us -> 86.2 us
    pallas_call x1, Pallas kernels: 102 us -> 86.2 us  [fused(): pl.pallas_call(kernel, out_shape=(jax.ShapeDtypeStruct((n, ch), BF16), ja...]
where the time goes in v2:
time: 91 us; the launch traced here: 90.8 us
  Pallas kernels  86.2 us (95%)
  local copies, waits for them, and re-layouts  3.95 us (4%)
    pallas_call x1, Pallas kernels, fused(): pl.pallas_call(kernel, out_shape=(jax.ShapeDtypeStruct((n, ch), BF16), ja...  86.2 us
    unnamed x7, local copies, waits for them, and re-layouts  3.95 us

profile of v2, /device:TPU:27, one launch (start us, length us, event | category | flops | bytes accessed | tf_op | source)
XLA Modules:
  0.0 90.8 jit_solution(13551119210874224210)
XLA Ops:
  0.6 86.2 %shard_map.76 = (bf16[512,512]{1,0:T(8,128)(2,1)}, f32[128,1024]{1,0:T(8,128)}, f32[128,1024]{1,0:T(8,128)}) custom-call(bf16[512,512]{1,0:T(8,128)(2,1)} %bitcast.6, f32[512,512]{1,0:T(8,128)} %bitcast.5, bf16[128,1024]{1,0:T(8,128)(2,1)} %w1_hbm.1, bf16[128,1024]{1,0:T(8,128)(2,1)} %w2_hbm.1, bf16[512,512]{1,0:T(8,128)(2,1)} %bitcast.7), custom_call_target="tpu_custom_call" | custom-call | flops 5368709120 | bytes 4194304 | tf_op jit(solution)/shard_map/pallas_call | solution.py:545
  86.8 0.0 copy-start.1
  86.8 1.9 %copy.11 = bf16[1,512,512]{2,1,0:T(8,128)(2,1)} copy(bf16[1,512,512]{2,1,0:T(8,128)(2,1)} %bitcast.4) | data formatting | bytes 1048576
  88.8 0.0 copy-done.1
  88.8 0.0 copy-start
  88.8 0.8 copy.12
  89.6 0.4 copy-done
  90.0 0.8 copy.13
Async XLA Ops:
  86.8 1.9 %copy-start.1 = (f32[128,1024]{1,0:T(8,128)S(1)}, f32[128,1024]{1,0:T(8,128)}, u32[]{:S(2)}) copy-start(f32[128,1024]{1,0:T(8,128)} %get-tuple-element.13) | copy-start | bytes 1572868
  88.8 1.2 %copy-start = (f32[128,1024]{1,0:T(8,128)S(1)}, f32[128,1024]{1,0:T(8,128)}, u32[]{:S(2)}) copy-start(f32[128,1024]{1,0:T(8,128)} %get-tuple-element.14) | copy-start | bytes 1572868

commit v3 on v2

--- a/solution.py
+++ b/solution.py
@@ -198,19 +198,55 @@
     def at_z(k):
         return lax.rem(z + k, Z) * 2 + y
 
-    along = [
-        [
-            hop(m, 0, k, wh.at[rows(place * q, q), :], quarter_of(w, f, place), t, at_z(k))
+    shards = (w1_hbm, w2_hbm)
+
+    def start_z(m):
+        return [
+            hop(m, 0, k, shards[m].at[rows(place * q, q), :],
+                quarter_of(weights[m], f, place), t, at_z(k))
             for k in range(1, Z)
         ]
-        for m, (wh, w) in enumerate(((w1_hbm, w1), (w2_hbm, w2)))
-    ]
-    first_y = [
-        hop(0, 2, 0, w1_hbm.at[rows(c * half_rows, half_rows), :], half_of(w1, f), t, over_y)
-    ]
-    second_y = [
-        hop(1, 1, 0, w2_hbm.at[rows(place * q, q), :], quarter_of(w2, f, place), t, over_y)
-    ]
+
+    def start_y(m):
+        return [
+            hop(m, 2, 0, shards[m].at[rows(c * half_rows, half_rows), :],
+                half_of(weights[m], f), t, over_y)
+        ]
+
+    def spread_xy(m, came_z, went_y):
+        went_x = []
+        for k in range(1, Z):
+            came_z[k - 1].wait_recv()
+            mine = quarter_of(weights[m], zone(k) * 2 + y, place)
+            went_x.append(hop(m, 1, k, mine, mine, across, f))
+            went_y.append(hop(m, 2, k, mine, mine, t, over_y))
+        return went_x
+
+    def spread_diagonal(m, went_y):
+        went = []
+        went_y[0].wait_recv()
+        for k in range(1, Z):
+            went_y[k].wait_recv()
+            mine = quarter_of(weights[m], zone(k) * 2 + 1 - y, place)
+            went.append(hop(m, 1, Z + k, mine, mine, across, f))
+        return went
+
+    def spread_core(m, went_x, diagonal):
+        went = []
+        for k in range(Z):
+            if k:
+                went_x[k - 1].wait_recv()
+                mine = half_of(weights[m], zone(k) * 2 + y)
+                went.append(hop(m, 3, k, mine, mine, sibling, f))
+                diagonal[k - 1].wait_recv()
+            mine = half_of(weights[m], zone(k) * 2 + 1 - y)
+            went.append(hop(m, 3, Z + k, mine, mine, sibling, f))
+        for copy in went:
+            copy.wait_recv()
+        own[m].wait()
+
+    first_z = start_z(0)
+    first_y = start_y(0)
 
     lanes = xs.shape[2]
     groups = ch // lanes
@@ -252,15 +288,9 @@
         send(ends.at[t], ends.at[t], es.at[k], er.at[k], lax.rem(t + k, T), f)
         for k in range(1, T)
     ]
-    first_x = []
-    for k in range(1, Z):
-        along[0][k - 1].wait_recv()
-        mine = quarter_of(w1, zone(k) * 2 + y, place)
-        first_x.append(hop(0, 1, k, mine, mine, across, f))
-    for k in range(1, Z):
-        along[1][k - 1].wait_recv()
-        mine = quarter_of(w2, zone(k) * 2 + y, place)
-        second_y.append(hop(1, 1, k, mine, mine, t, over_y))
+    first_x = spread_xy(0, first_z, first_y)
+    second_z = start_z(1)
+    second_y = start_y(1)
     for copy in states:
         copy.wait_recv()
     carried = jnp.zeros((1, ch), F32)
@@ -291,26 +321,9 @@
     pl.when(has_next)(tail.start)
     x1[lag:, :ch] = x1[: frames_n - lag, ch:]
 
-    first_core, second_x, second_core = [], [], []
-    for k in range(1, Z):
-        first_x[k - 1].wait_recv()
-        mine = half_of(w1, zone(k) * 2 + y)
-        first_y.append(hop(0, 2, k, mine, mine, t, over_y))
-        first_core.append(hop(0, 3, k, mine, mine, sibling, f))
-    for k in range(1, Z):
-        mine = quarter_of(w2, zone(k) * 2 + y, place)
-        second_x.append(hop(1, 2, k, mine, mine, across, f))
-    for k in range(Z):
-        second_y[k].wait_recv()
-        mine = quarter_of(w2, zone(k) * 2 + 1 - y, place)
-        second_x.append(hop(1, 2, Z + k, mine, mine, across, f))
-    for k in range(Z):
-        first_y[k].wait_recv()
-        mine = half_of(w1, zone(k) * 2 + 1 - y)
-        first_core.append(hop(0, 3, Z + k, mine, mine, sibling, f))
-    for copy in first_core:
-        copy.wait_recv()
-    own[0].wait()
+    first_diagonal = spread_diagonal(0, first_y)
+    second_x = spread_xy(1, second_z, second_y)
+    spread_core(0, first_x, first_diagonal)
 
     @pl.when(has_prev)
     def _():
@@ -350,19 +363,13 @@
         def _():
             passed(r).start()
 
-    for k in range(2 * Z - 1):
-        second_x[k].wait_recv()
-        owner = zone(k + 1) * 2 + y if k < Z - 1 else zone(k - Z + 1) * 2 + 1 - y
-        mine = half_of(w2, owner)
-        second_core.append(hop(1, 3, k, mine, mine, sibling, f))
+    second_diagonal = spread_diagonal(1, second_y)
 
     @pl.when(t == 0)
     def _():
         prev_out[...] = jnp.zeros((frames_n, ch), BF16)
 
-    for copy in second_core:
-        copy.wait_recv()
-    own[1].wait()
+    spread_core(1, second_x, second_diagonal)
 
     @pl.loop(0, frames_n, step=block)
     def _(r):
@@ -414,23 +421,23 @@
         for j in range(h * two, (h + 1) * two):
             for d in range(2):
                 for e in range(2):
-                    yy, xx = (d, e) if m == 0 else (e, d)
+                    yy, xx = (d, e) if h == 0 else (e, d)
                     core_sum[m, d, j, e] = (
                         part[m, j, yy, c, xx].astype(F32) + core_in[m, j, yy, xx].astype(F32)
                     ).astype(BF16)
-        mine, tm, fsdp = (y, t, over_y) if m == 0 else (x, across, f)
+        mine, tm, fsdp = (y, t, over_y) if h == 0 else (x, across, f)
         return send(core_sum.at[m, 1 - mine, span(h)], a_in.at[m, span(h)],
                     ss.at[m, 1, h], sr.at[m, 1, h], tm, fsdp)
 
     def b_phase(m, h, copy):
         copy.wait_recv()
-        mine = y if m == 0 else x
+        mine = y if h == 0 else x
         for j in range(h * two, (h + 1) * two):
             for e in range(2):
                 a_sum[m, e, j] = (
                     core_sum[m, mine, j, e].astype(F32) + a_in[m, j, e].astype(F32)
                 ).astype(BF16)
-        mine, tm, fsdp = (x, across, f) if m == 0 else (y, t, over_y)
+        mine, tm, fsdp = (x, across, f) if h == 0 else (y, t, over_y)
         return send(a_sum.at[m, 1 - mine, span(h)], b_in.at[m, span(h)],
                     ss.at[m, 2, h], sr.at[m, 2, h], tm, fsdp)
 
@@ -443,7 +450,7 @@
 
     def z_phase(m, h, copy):
         copy.wait_recv()
-        mine = x if m == 0 else y
+        mine = x if h == 0 else y
         for j in range(h * two, (h + 1) * two):
             b_sum[m, j] = (
                 a_sum[m, mine, j].astype(F32) + b_in[m, j].astype(F32)
@@ -512,9 +519,9 @@
     b20 = b_phase(0, 0, a20)
     b21 = b_phase(0, 1, a21)
     b10 = b_phase(1, 0, a10)
+    b11 = b_phase(1, 1, a11)
     z_phase(0, 0, b20)
     z_phase(0, 1, b21)
-    b11 = b_phase(1, 1, a11)
     z_phase(1, 0, b10)
     z_phase(1, 1, b11)
     last2 = q_phase(0)

time: 91 us -> 86.3 us (0.948)
  Pallas kernels: 86.2 us -> 80.6 us
    pallas_call x1, Pallas kernels: 86.2 us -> 80.6 us  [fused(): pl.pallas_call(kernel, out_shape=(jax.ShapeDtypeStruct((n, ch), BF16), ja...]
where the time goes in v3:
time: 86.3 us; the launch traced here: 85.2 us
  Pallas kernels  80.6 us (93%)
  local copies, waits for them, and re-layouts  3.95 us (5%)
    pallas_call x1, Pallas kernels, fused(): pl.pallas_call(kernel, out_shape=(jax.ShapeDtypeStruct((n, ch), BF16), ja...  80.6 us
    unnamed x7, local copies, waits for them, and re-layouts  3.95 us

profile of v3, /device:TPU:27, one launch (start us, length us, event | category | flops | bytes accessed | tf_op | source)
XLA Modules:
  0.0 85.2 jit_solution(9009325474352215783)
XLA Ops:
  0.6 80.6 %shard_map.76 = (bf16[512,512]{1,0:T(8,128)(2,1)}, f32[128,1024]{1,0:T(8,128)}, f32[128,1024]{1,0:T(8,128)}) custom-call(bf16[512,512]{1,0:T(8,128)(2,1)} %bitcast.6, f32[512,512]{1,0:T(8,128)} %bitcast.5, bf16[128,1024]{1,0:T(8,128)(2,1)} %w1_hbm.1, bf16[128,1024]{1,0:T(8,128)(2,1)} %w2_hbm.1, bf16[512,512]{1,0:T(8,128)(2,1)} %bitcast.7), custom_call_target="tpu_custom_call" | custom-call | flops 5368709120 | bytes 4194304 | tf_op jit(solution)/shard_map/pallas_call | solution.py:552
  81.2 0.0 copy-start.1
  81.2 1.9 %copy.11 = bf16[1,512,512]{2,1,0:T(8,128)(2,1)} copy(bf16[1,512,512]{2,1,0:T(8,128)(2,1)} %bitcast.4) | data formatting | bytes 1048576
  83.2 0.0 copy-done.1
  83.2 0.0 copy-start
  83.2 0.8 copy.12
  84.0 0.4 copy-done
  84.4 0.8 copy.13
Async XLA Ops:
  81.2 1.9 %copy-start.1 = (f32[128,1024]{1,0:T(8,128)S(1)}, f32[128,1024]{1,0:T(8,128)}, u32[]{:S(2)}) copy-start(f32[128,1024]{1,0:T(8,128)} %get-tuple-element.13) | copy-start | bytes 1572868
  83.2 1.2 %copy-start = (f32[128,1024]{1,0:T(8,128)S(1)}, f32[128,1024]{1,0:T(8,128)}, u32[]{:S(2)}) copy-start(f32[128,1024]{1,0:T(8,128)} %get-tuple-element.14) | copy-start | bytes 1572868

commit v4 on v3

--- a/solution.py
+++ b/solution.py
@@ -482,6 +482,7 @@
     partial(0, out1, half)
     core21 = core_phase(0, 1)
     a20 = a_phase(0, 0, core20)
+    a21 = a_phase(0, 1, core21)
 
     @pl.loop(0, frames_n, step=block)
     def _(r):
@@ -489,8 +490,6 @@
         pre2[at, :] = cot[at, :].astype(F32) + lax.dot_general(
             g[0, at, :], w2[ch:, :], (((1,), (1,)), ((), ())), preferred_element_type=F32
         )
-
-    a21 = a_phase(0, 1, core21)
 
     @pl.when(t == T - 1)
     def _():

time: 86.3 us -> 84.6 us (0.980)
  Pallas kernels: 80.6 us -> 78.7 us
    pallas_call x1, Pallas kernels: 80.6 us -> 78.7 us  [fused(): pl.pallas_call(kernel, out_shape=(jax.ShapeDtypeStruct((n, ch), BF16), ja...]
where the time goes in v4:
time: 84.6 us; the launch traced here: 83.3 us
  Pallas kernels  78.7 us (93%)
  local copies, waits for them, and re-layouts  3.95 us (5%)
    pallas_call x1, Pallas kernels, fused(): pl.pallas_call(kernel, out_shape=(jax.ShapeDtypeStruct((n, ch), BF16), ja...  78.7 us
    unnamed x7, local copies, waits for them, and re-layouts  3.95 us

profile of v4, /device:TPU:27, one launch (start us, length us, event | category | flops | bytes accessed | tf_op | source)
XLA Modules:
  0.0 83.3 jit_solution(11645588168014324031)
XLA Ops:
  0.6 78.7 %shard_map.76 = (bf16[512,512]{1,0:T(8,128)(2,1)}, f32[128,1024]{1,0:T(8,128)}, f32[128,1024]{1,0:T(8,128)}) custom-call(bf16[512,512]{1,0:T(8,128)(2,1)} %bitcast.6, f32[512,512]{1,0:T(8,128)} %bitcast.5, bf16[128,1024]{1,0:T(8,128)(2,1)} %w1_hbm.1, bf16[128,1024]{1,0:T(8,128)(2,1)} %w2_hbm.1, bf16[512,512]{1,0:T(8,128)(2,1)} %bitcast.7), custom_call_target="tpu_custom_call" | custom-call | flops 5368709120 | bytes 4194304 | tf_op jit(solution)/shard_map/pallas_call | solution.py:551
  79.3 0.0 copy-start.1
  79.3 1.9 %copy.11 = bf16[1,512,512]{2,1,0:T(8,128)(2,1)} copy(bf16[1,512,512]{2,1,0:T(8,128)(2,1)} %bitcast.4) | data formatting | bytes 1048576
  81.3 0.0 copy-done.1
  81.3 0.0 copy-start
  81.3 0.8 copy.12
  82.1 0.4 copy-done
  82.5 0.8 copy.13
Async XLA Ops:
  79.3 1.9 %copy-start.1 = (f32[128,1024]{1,0:T(8,128)S(1)}, f32[128,1024]{1,0:T(8,128)}, u32[]{:S(2)}) copy-start(f32[128,1024]{1,0:T(8,128)} %get-tuple-element.13) | copy-start | bytes 1572868
  81.3 1.2 %copy-start = (f32[128,1024]{1,0:T(8,128)S(1)}, f32[128,1024]{1,0:T(8,128)}, u32[]{:S(2)}) copy-start(f32[128,1024]{1,0:T(8,128)} %get-tuple-element.14) | copy-start | bytes 1572868
